TPU v7x, 512 devices: a whole 4x8x8 slice. The times are simulated.
512 devices in a mesh: dp: 64 (over y_hi, x, z), mp: 8 (over y_lo, core).
Axes of the slice: x: 4, y: 8 (y_hi: 2, y_lo: 4; y = y_hi * 4 + y_lo), z: 8, core: 2. Of those that a mesh axis runs over, the one named last changes fastest.
Arguments:
- inputs: bfloat16 [106496, 8192], P('dp', 'mp'), may hold values from -16 to 16
- out_grad: bfloat16 [106496, 512], P('dp'), may hold values from -0.018310547 to 0.018310547
- weight: float32 [8192, 512], P(('mp', 'dp')), may hold values from -8 to 8
- row_moment: float32 [8192], P(('mp', 'dp')), may hold values from 0.015 to 1.5
- col_moment: float32 [512], replicated, may hold values from 0.03 to 1
Outputs:
- new_weight: float32 [8192, 512], P(('mp', 'dp'))
- new_rows: float32 [8192], P(('mp', 'dp'))
- new_cols: float32 [512], replicated
All inputs are finite; a program needn't handle non-finite values.
Results may differ from a plain program's by a relative error of at most 0.0003.
Values sent between devices are 32-bit elements; how exact they have to be, the bound alone decides.
No kernel may reach another device: no remote copies, remote signals or barrier semaphores. Data moves between devices by JAX's collectives and lax.ppermute only.
A program may use at most 64 MiB of HBM per device.

v0:
```python
import jax
import jax.numpy as jnp
from jax import lax
from jax.experimental import pallas as pl
from jax.experimental.pallas import tpu as pltpu
from jax.sharding import Mesh, PartitionSpec as P

D = 8192
WIDTH = 512
ROWS = 16
LANES = 128
MIB = 1024 * 1024
AXES = ("yh", "x", "z", "yl", "c")
SIZES = (2, 4, 8, 4, 2)
DP = ("yh", "x", "z")
MP = ("yl", "c")
SMALL = 2 * WIDTH + 2 * LANES
MOMENTS = 2 * ROWS
SQUARES = MOMENTS + 1
CARRIED = 2 * ROWS + 8


CLASS_X = ((1, 2), (0, 3))
CLASS_Z = ((1, 3, 4, 6), (0, 2, 5, 7))
BLOCKS_X = ((0, 1), (2, 3))
BLOCKS_Z = ((0, 1), (2, 3), (4, 5), (6, 7))


def place(yh, x, z, yl, c):
    return (((yh * 4 + (x + c) % 4) * 8 + (z + c) % 8) * 4 + yl) * 2 + c


def near_groups():
    return [
        [
            place(yh, next(x for x in xs if x in class_x), next(z for z in zs if z in class_z), yl, c)
            for class_x in CLASS_X
            for class_z in CLASS_Z
        ]
        for yh in range(2)
        for xs in BLOCKS_X
        for zs in BLOCKS_Z
        for yl in range(4)
        for c in range(2)
    ]


def far_groups():
    return [
        [place(yh, x, z, yl, c) for x in class_x for z in class_z]
        for class_x in CLASS_X
        for class_z in CLASS_Z
        for yh in range(2)
        for yl in range(4)
        for c in range(2)
    ]


def position(yh, x, z, core):
    x, z = (x - core) % 4, (z - core) % 8
    kx = next(k for k, xs in enumerate(CLASS_X) if x in xs)
    kz = next(k for k, zs in enumerate(CLASS_Z) if z in zs)
    return 2 * kx + kz, (CLASS_X[kx].index(x) * 4 + CLASS_Z[kz].index(z)) * 2 + yh


CHUNKS = (512, 512, 640)
BLOCKS = 4
HERE = pl.BlockSpec(memory_space=pltpu.VMEM)


def in_vmem(array):
    return pltpu.with_memory_space_constraint(array, pltpu.VMEM)


def in_hbm(array):
    return pltpu.with_memory_space_constraint(array, pltpu.HBM)


def product_kernel(inputs_ref, columns_ref, out_ref, inputs, columns, total, in_sems, column_sems):
    core = lax.axis_index("c")
    copies = []
    first = 0
    for i, tokens in enumerate(CHUNKS):
        span = pl.ds(first, tokens)
        pair = (
            pltpu.make_async_copy(columns_ref.at[span], columns.at[span], column_sems.at[i]),
            pltpu.make_async_copy(inputs_ref.at[span], inputs.at[span], in_sems.at[i]),
        )
        for copy in pair:
            copy.start()
        copies.append((first, tokens, pair))
        first += tokens
    size = inputs.shape[1] // BLOCKS
    for i, (first, tokens, pair) in enumerate(copies):
        for copy in pair:
            copy.wait()
        for block in range(BLOCKS):
            rows = slice(block * size, (block + 1) * size)
            product = lax.dot_general(
                inputs[first : first + tokens, rows],
                columns[first : first + tokens],
                (((0,), (0,)), ((), ())),
                preferred_element_type=jnp.float32,
            )
            if i > 0:
                product = product + total[rows]
            if i < len(CHUNKS) - 1:
                total[rows] = product
                continue
            for r in range(size // ROWS):
                device = block * (size // ROWS) + r
                where = device // 32, device // 8 % 4, device % 8
                (kind, index), (kind1, index1) = position(*where, 0), position(*where, 1)
                kind, index = kind + core * (kind1 - kind), index + core * (index1 - index)
                out_ref[kind, index] = product[r * ROWS : (r + 1) * ROWS]


def token_product(inputs, out_grad):
    tokens, rows = inputs.shape
    return pl.pallas_call(
        product_kernel,
        in_specs=[pl.BlockSpec(memory_space=pl.ANY)] * 2,
        out_specs=HERE,
        out_shape=pltpu.VMEM((4, 16, ROWS, WIDTH), jnp.float32),
        scratch_shapes=[
            pltpu.VMEM((tokens, rows), jnp.bfloat16),
            pltpu.VMEM((tokens, WIDTH), jnp.bfloat16),
            pltpu.VMEM((rows, WIDTH), jnp.float32),
            pltpu.SemaphoreType.DMA((len(CHUNKS),)),
            pltpu.SemaphoreType.DMA((len(CHUNKS),)),
        ],
        compiler_params=pltpu.CompilerParams(vmem_limit_bytes=24 * MIB),
    )(in_hbm(inputs), in_hbm(out_grad))


def diagonal():
    return lax.broadcasted_iota(jnp.int32, (ROWS, ROWS), 0) == lax.broadcasted_iota(jnp.int32, (ROWS, ROWS), 1)


def to_column(row):
    return jnp.sum(jnp.where(diagonal(), row, 0.0), axis=1, keepdims=True)


def to_row(column):
    return jnp.sum(jnp.where(diagonal(), column, 0.0), axis=0, keepdims=True)


def pack_kernel(parts_ref, weight_ref, row_moment_ref, out_ref):
    total = jnp.sum(parts_ref[...], axis=0)
    for half in range(2):
        out_ref[half * ROWS : (half + 1) * ROWS] = total[half]
    out_ref[MOMENTS:] = jnp.zeros((CARRIED - MOMENTS, WIDTH), jnp.float32)
    out_ref[MOMENTS : MOMENTS + 1, :ROWS] = row_moment_ref[...]
    out_ref[SQUARES : SQUARES + 1] = jnp.sum(weight_ref[...] * weight_ref[...], axis=0, keepdims=True)


def pack(parts, weight, row_moment):
    return pl.pallas_call(
        pack_kernel,
        in_specs=[HERE] * 3,
        out_specs=HERE,
        out_shape=pltpu.VMEM((CARRIED, WIDTH), jnp.float32),
    )(in_vmem(parts), in_vmem(weight), in_vmem(row_moment))


def statistics_kernel(mine_ref, other_ref, grad_ref, rows_ref, small_ref):
    half = lax.axis_index("yh")

    def rows_of(which, moments_ref):
        span = pl.ds(pl.multiple_of(which * ROWS, ROWS), ROWS)
        grad = mine_ref[span, :] + other_ref[span, :]
        squares = grad * grad
        moments = to_column(moments_ref[MOMENTS : MOMENTS + 1, :ROWS])
        new_rows = 0.9 * moments + 0.1 * (jnp.sum(squares, axis=1, keepdims=True) / WIDTH)
        plain = jnp.sum(squares, axis=0, keepdims=True)
        scaled = jnp.sum(squares / new_rows, axis=0, keepdims=True)
        return grad, to_row(new_rows), plain, scaled

    grad, new_rows, plain, scaled = rows_of(half, mine_ref)
    _, far_rows, far_plain, far_scaled = rows_of(1 - half, other_ref)
    grad_ref[...] = grad
    rows_ref[...] = new_rows
    weight_squares = mine_ref[SQUARES : SQUARES + 1] + other_ref[SQUARES : SQUARES + 1]
    small_ref[:, :WIDTH] = plain + far_plain
    small_ref[:, WIDTH : 2 * WIDTH] = scaled + far_scaled
    small_ref[:, 2 * WIDTH : 2 * WIDTH + LANES] = sum(
        weight_squares[:, i : i + LANES] for i in range(0, WIDTH, LANES)
    )
    small_ref[:, 2 * WIDTH + LANES :] = jnp.zeros((1, LANES), jnp.float32)
    small_ref[:, 2 * WIDTH + LANES : 2 * WIDTH + LANES + ROWS] = new_rows + far_rows


def statistics(mine, other):
    return pl.pallas_call(
        statistics_kernel,
        in_specs=[HERE] * 2,
        out_specs=(HERE,) * 3,
        out_shape=(
            pltpu.VMEM((ROWS, WIDTH), jnp.float32),
            pltpu.VMEM((1, ROWS), jnp.float32),
            pltpu.VMEM((1, SMALL), jnp.float32),
        ),
    )(in_vmem(mine), in_vmem(other))


def update_kernel(small_ref, grad_ref, rows_ref, weight_ref, col_moment_ref, new_weight_ref, new_rows_ref, new_cols_ref):
    new_rows_ref[...] = rows_ref[...]
    small = jnp.sum(small_ref[...], axis=0)
    column_sum, scaled_sum = small[:, :WIDTH], small[:, WIDTH : 2 * WIDTH]
    weight_total = jnp.sum(small[:, 2 * WIDTH : 2 * WIDTH + LANES], axis=1, keepdims=True)
    row_mean = jnp.sum(small[:, 2 * WIDTH + LANES :], axis=1, keepdims=True) / D
    new_cols = 0.9 * col_moment_ref[...] + 0.1 * (column_sum / D)
    new_cols_ref[...] = new_cols
    update_total = row_mean * jnp.sum(scaled_sum / new_cols, axis=1, keepdims=True)
    new_rows = to_column(rows_ref[...])
    update = grad_ref[...] * lax.rsqrt(new_rows * new_cols / row_mean)
    entries = D * WIDTH
    update_rms = jnp.sqrt(update_total / entries)
    weight_rms = jnp.sqrt(weight_total / entries + 1e-06)
    factor = 0.05 * weight_rms / jnp.maximum(jnp.float32(1.0), update_rms)
    new_weight_ref[...] = weight_ref[...] - factor * update


def apply_update(small, grad, new_rows, weight, col_moment):
    return pl.pallas_call(
        update_kernel,
        in_specs=[HERE] * 5,
        out_specs=(HERE,) * 3,
        out_shape=(
            jax.ShapeDtypeStruct((ROWS, WIDTH), jnp.float32),
            jax.ShapeDtypeStruct((1, ROWS), jnp.float32),
            jax.ShapeDtypeStruct((1, WIDTH), jnp.float32),
        ),
    )(*(in_vmem(array) for array in (small, grad, new_rows, weight, col_moment)))


def copies_of(value, axes, count):
    return lax.all_to_all(jnp.broadcast_to(value[None], (count,) + value.shape), axes, 0, 0, tiled=True)


def body(inputs, out_grad, weight, row_moment, col_moment):
    parts = token_product(inputs, out_grad)
    parts = lax.all_to_all(parts, AXES, 0, 0, tiled=True, axis_index_groups=near_groups())
    parts = jnp.sum(parts, axis=0).reshape(8, 2, ROWS, WIDTH)
    parts = lax.all_to_all(parts, AXES, 0, 0, tiled=True, axis_index_groups=far_groups())
    mine = pack(parts, weight, row_moment.reshape(1, ROWS))
    other = lax.ppermute(mine, "yh", [(0, 1), (1, 0)])
    grad, row_values, small = statistics(mine, other)
    small = jnp.sum(copies_of(small, ("yl", "c"), 8), axis=0)
    small = copies_of(small, ("x", "z"), 32)
    new_weight, new_rows, new_cols = apply_update(small, grad, row_values, weight, col_moment.reshape(1, WIDTH))
    return (new_weight, new_rows.reshape(ROWS), new_cols.reshape(WIDTH))


def solution(mesh):
    fine = Mesh(mesh.devices.reshape(SIZES), AXES)
    placed = (P(DP, MP), P(DP, None), P(MP + DP, None), P(MP + DP), P())
    return jax.shard_map(
        body,
        mesh=fine,
        in_specs=placed,
        out_specs=(P(MP + DP, None), P(MP + DP), P()),
        check_vma=False,
    )
```

profile of v0, /device:TPU:1, one launch (start us, length us, event | category | flops | bytes accessed | tf_op | source)
XLA Modules:
  0.0 87.6 jit_solution(14063793953340480383)
XLA Ops:
  0.6 3.7 %shard_map.76 = f32[4,16,16,512]{3,2,1,0:T(8,128)S(1)} custom-call(bf16[1664,1024]{1,0:T(8,128)(2,1)} %inputs_ref.1, bf16[1664,512]{1,0:T(8,128)(2,1)} %columns_ref.1), custom_call_target="tpu_custom_call" | custom-call | tf_op jit(solution)/shard_map/pallas_call | solution.py:120
  4.3 26.9 %all_to_all.20 = f32[4,16,16,512]{3,2,1,0:T(8,128)S(1)} all-to-all(f32[4,16,16,512]{3,2,1,0:T(8,128)S(1)} %shard_map.76), channel_id=1, replica_groups={{72,64,8,0},{145,137,81,73},{74,66,10,2},{147,139,83,75},{76,68,12,4},{..., dimensions={0} | all-to-all | bytes 4194304 | tf_op jit(solution)/shard_map/all_to_all | solution.py:243
  31.3 0.0 copy-start
  31.3 0.0 copy-start.2
  31.3 0.0 copy-start.1
  31.3 0.3 reduce_sum.18
  31.5 14.2 %all_to_all.21.parts_ref = f32[8,2,16,512]{3,2,1,0:T(8,128)S(1)} all-to-all(f32[8,2,16,512]{3,2,1,0:T(8,128)S(1)} %bitcast.7), channel_id=1, replica_groups={{72,88,96,112,136,152,160,176},{145,161,169,185,209,225,233,249},{74,90..., dimensions={0} | all-to-all | bytes 1048576 | tf_op jit(solution)/shard_map/all_to_all | solution.py:245
  45.7 0.0 copy-done
  45.7 0.0 copy-done.2
  45.8 7.4 %collective-permute-start = (f32[40,512]{1,0:T(8,128)S(1)}, f32[40,512]{1,0:T(8,128)S(1)}, u32[]{:S(2)}, u32[]{:S(2)}) collective-permute-start(f32[40,512]{1,0:T(8,128)S(1)} %shard_map.77.mine_ref), channel_id=1, source_target_pairs={{0,256},{256,0},{1,257},{257,1},{2,258},{258,2},{3,259},{259,3},{4... | collective-permute-start | bytes 245768 | tf_op jit(solution)/shard_map/ppermute | solution.py:247
  53.2 1.9 %collective-permute-done.other_ref = f32[40,512]{1,0:T(8,128)S(1)} collective-permute-done((f32[40,512]{1,0:T(8,128)S(1)}, f32[40,512]{1,0:T(8,128)S(1)}, u32[]{:S(2)}, u32[]{:S(2)}) %collective-permute-start) | collective-permute-done | bytes 81952 | tf_op jit(solution)/shard_map/ppermute | solution.py:247
  55.1 0.1 shard_map.78
  55.3 16.9 %all_to_all.22 = f32[8,1,1280]{2,1,0:T(1,128)S(1)} all-to-all(f32[8,1,1280]{2,1,0:T(1,128)S(1)} %broadcast_in_dim.7), channel_id=1, replica_groups=mesh['yh'=2,'x'=4,'z'=8,'yl'=4,'c'=2] {'yl','c'}, dimensions={0} | all-to-all | bytes 81920 | tf_op jit(solution)/shard_map/all_to_all | solution.py:238
  72.2 0.1 broadcast_in_dim.16
  72.3 14.4 %all_to_all.23.small_ref = f32[32,1,1280]{2,1,0:T(1,128)S(1)} all-to-all(f32[32,1,1280]{2,1,0:T(1,128)S(1)} %broadcast_in_dim.16), channel_id=1, replica_groups=mesh['yh'=2,'x'=4,'z'=8,'yl'=4,'c'=2] {'x','z'}, dimensions={0} | all-to-all | bytes 327680 | tf_op jit(solution)/shard_map/all_to_all | solution.py:238
  86.7 0.0 copy-done.1
  86.7 0.8 shard_map.79
  (4 shorter events, 0.1 us)
Async XLA Ops:
  31.3 14.4 %copy-start = (f32[16,512]{1,0:T(8,128)S(1)}, f32[16,512]{1,0:T(8,128)}, u32[]{:S(2)}) copy-start(f32[16,512]{1,0:T(8,128)} %weight_ref.3) | copy-start | bytes 98308
  31.3 14.4 %copy-start.2 = (f32[16]{0:T(128)S(1)}, f32[16]{0:T(128)}, u32[]{:S(2)}) copy-start(f32[16]{0:T(128)} %param.8) | copy-start | bytes 196
  31.3 55.4 %copy-start.1 = (f32[512]{0:T(512)S(1)}, f32[512]{0:T(512)}, u32[]{:S(2)}) copy-start(f32[512]{0:T(512)} %param.9) | copy-start | bytes 6148
  45.8 9.3 %collective-permute-start = (f32[40,512]{1,0:T(8,128)S(1)}, f32[40,512]{1,0:T(8,128)S(1)}, u32[]{:S(2)}, u32[]{:S(2)}) collective-permute-start(f32[40,512]{1,0:T(8,128)S(1)} %shard_map.77.mine_ref), channel_id=1, source_target_pairs={{0,256},{256,0},{1,257},{257,1},{2,258},{258,2},{3,259},{259,3},{4... | collective-permute-start | bytes 245768 | tf_op jit(solution)/shard_map/ppermute | solution.py:247
where the time goes:
time: 87.9 us; the launch traced here: 87.6 us
  blocking collectives  72.4 us (82%)
  starting transfers between devices  7.41 us (8%)
  Pallas kernels  4.71 us (5%)
  waiting for transfers between devices  1.9 us (2%)
    all_to_all x2, blocking collectives, copies_of(): lax.all_to_all(jnp.broadcast_to(value[None], (count,) + value.shape), axe...  31.3 us
    all_to_all x1, blocking collectives, body(): lax.all_to_all(parts, AXES, 0, 0, tiled=True, axis_index_groups=near_grou...  26.9 us
    all_to_all x1, blocking collectives, body(): lax.all_to_all(parts, AXES, 0, 0, tiled=True, axis_index_groups=far_group...  14.2 us
    ppermute x1, starting transfers between devices, body(): other = lax.ppermute(mine, 'yh', [(0, 1), (1, 0)])  7.41 us
    pallas_call x1, Pallas kernels, token_product(): pl.pallas_call(product_kernel, in_specs=[pl.BlockSpec(memory_space=pl.ANY...  3.71 us
    ppermute x1, waiting for transfers between devices, body(): other = lax.ppermute(mine, 'yh', [(0, 1), (1, 0)])  1.9 us
  transfers between devices with their start and end apart: 1, of which 1 were waited for; matrix products, arithmetic and copies ran while one was open for 0% of the time, Pallas kernels for 0%

commit v1 on v0

--- a/solution.py
+++ b/solution.py
@@ -14,7 +14,8 @@
 SIZES = (2, 4, 8, 4, 2)
 DP = ("yh", "x", "z")
 MP = ("yl", "c")
-SMALL = 2 * WIDTH + 2 * LANES
+SMALL = 2 * WIDTH + LANES
+HALF = LANES // 2
 MOMENTS = 2 * ROWS
 SQUARES = MOMENTS + 1
 CARRIED = 2 * ROWS + 8
@@ -183,11 +184,9 @@
     weight_squares = mine_ref[SQUARES : SQUARES + 1] + other_ref[SQUARES : SQUARES + 1]
     small_ref[:, :WIDTH] = plain + far_plain
     small_ref[:, WIDTH : 2 * WIDTH] = scaled + far_scaled
-    small_ref[:, 2 * WIDTH : 2 * WIDTH + LANES] = sum(
-        weight_squares[:, i : i + LANES] for i in range(0, WIDTH, LANES)
-    )
-    small_ref[:, 2 * WIDTH + LANES :] = jnp.zeros((1, LANES), jnp.float32)
-    small_ref[:, 2 * WIDTH + LANES : 2 * WIDTH + LANES + ROWS] = new_rows + far_rows
+    small_ref[:, 2 * WIDTH :] = jnp.zeros((1, LANES), jnp.float32)
+    small_ref[:, 2 * WIDTH : 2 * WIDTH + HALF] = sum(weight_squares[:, i : i + HALF] for i in range(0, WIDTH, HALF))
+    small_ref[:, 2 * WIDTH + HALF : 2 * WIDTH + HALF + ROWS] = new_rows + far_rows
 
 
 def statistics(mine, other):
@@ -207,8 +206,8 @@
     new_rows_ref[...] = rows_ref[...]
     small = jnp.sum(small_ref[...], axis=0)
     column_sum, scaled_sum = small[:, :WIDTH], small[:, WIDTH : 2 * WIDTH]
-    weight_total = jnp.sum(small[:, 2 * WIDTH : 2 * WIDTH + LANES], axis=1, keepdims=True)
-    row_mean = jnp.sum(small[:, 2 * WIDTH + LANES :], axis=1, keepdims=True) / D
+    weight_total = jnp.sum(small[:, 2 * WIDTH : 2 * WIDTH + HALF], axis=1, keepdims=True)
+    row_mean = jnp.sum(small[:, 2 * WIDTH + HALF :], axis=1, keepdims=True) / D
     new_cols = 0.9 * col_moment_ref[...] + 0.1 * (column_sum / D)
     new_cols_ref[...] = new_cols
     update_total = row_mean * jnp.sum(scaled_sum / new_cols, axis=1, keepdims=True)

time: 87.9 us -> 87.8 us (level)
  no operation moved by 1% of the time
where the time goes in v1:
time: 87.8 us; the launch traced here: 87.5 us
  blocking collectives  72.3 us (82%)
  starting transfers between devices  7.41 us (8%)
  Pallas kernels  4.76 us (5%)
  waiting for transfers between devices  1.9 us (2%)
    all_to_all x2, blocking collectives, copies_of(): lax.all_to_all(jnp.broadcast_to(value[None], (count,) + value.shape), axe...  31.2 us
    all_to_all x1, blocking collectives, body(): lax.all_to_all(parts, AXES, 0, 0, tiled=True, axis_index_groups=near_grou...  26.9 us
    all_to_all x1, blocking collectives, body(): lax.all_to_all(parts, AXES, 0, 0, tiled=True, axis_index_groups=far_group...  14.2 us
    ppermute x1, starting transfers between devices, body(): other = lax.ppermute(mine, 'yh', [(0, 1), (1, 0)])  7.41 us
    pallas_call x1, Pallas kernels, token_product(): pl.pallas_call(product_kernel, in_specs=[pl.BlockSpec(memory_space=pl.ANY...  3.71 us
    ppermute x1, waiting for transfers between devices, body(): other = lax.ppermute(mine, 'yh', [(0, 1), (1, 0)])  1.9 us
  transfers between devices with their start and end apart: 1, of which 1 were waited for; matrix products, arithmetic and copies ran while one was open for 0% of the time, Pallas kernels for 0%

profile of v1, /device:TPU:1, one launch (start us, length us, event | category | flops | bytes accessed | tf_op | source)
XLA Modules:
  0.0 87.5 jit_solution(4421533090966812668)
XLA Ops:
  0.6 3.7 %shard_map.76 = f32[4,16,16,512]{3,2,1,0:T(8,128)S(1)} custom-call(bf16[1664,1024]{1,0:T(8,128)(2,1)} %inputs_ref.1, bf16[1664,512]{1,0:T(8,128)(2,1)} %columns_ref.1), custom_call_target="tpu_custom_call" | custom-call | tf_op jit(solution)/shard_map/pallas_call | solution.py:121
  4.3 26.9 %all_to_all.20 = f32[4,16,16,512]{3,2,1,0:T(8,128)S(1)} all-to-all(f32[4,16,16,512]{3,2,1,0:T(8,128)S(1)} %shard_map.76), channel_id=1, replica_groups={{72,64,8,0},{145,137,81,73},{74,66,10,2},{147,139,83,75},{76,68,12,4},{..., dimensions={0} | all-to-all | bytes 4194304 | tf_op jit(solution)/shard_map/all_to_all | solution.py:242
  31.3 0.0 copy-start
  31.3 0.0 copy-start.2
  31.3 0.0 copy-start.1
  31.3 0.3 reduce_sum.18
  31.5 14.2 %all_to_all.21.parts_ref = f32[8,2,16,512]{3,2,1,0:T(8,128)S(1)} all-to-all(f32[8,2,16,512]{3,2,1,0:T(8,128)S(1)} %bitcast.7), channel_id=1, replica_groups={{72,88,96,112,136,152,160,176},{145,161,169,185,209,225,233,249},{74,90..., dimensions={0} | all-to-all | bytes 1048576 | tf_op jit(solution)/shard_map/all_to_all | solution.py:244
  45.7 0.0 copy-done
  45.7 0.0 copy-done.2
  45.8 7.4 %collective-permute-start = (f32[40,512]{1,0:T(8,128)S(1)}, f32[40,512]{1,0:T(8,128)S(1)}, u32[]{:S(2)}, u32[]{:S(2)}) collective-permute-start(f32[40,512]{1,0:T(8,128)S(1)} %shard_map.77.mine_ref), channel_id=1, source_target_pairs={{0,256},{256,0},{1,257},{257,1},{2,258},{258,2},{3,259},{259,3},{4... | collective-permute-start | bytes 245768 | tf_op jit(solution)/shard_map/ppermute | solution.py:246
  53.2 1.9 %collective-permute-done.other_ref = f32[40,512]{1,0:T(8,128)S(1)} collective-permute-done((f32[40,512]{1,0:T(8,128)S(1)}, f32[40,512]{1,0:T(8,128)S(1)}, u32[]{:S(2)}, u32[]{:S(2)}) %collective-permute-start) | collective-permute-done | bytes 81952 | tf_op jit(solution)/shard_map/ppermute | solution.py:246
  55.1 0.2 shard_map.78
  55.3 16.9 %all_to_all.22 = f32[8,1,1152]{2,1,0:T(1,128)S(1)} all-to-all(f32[8,1,1152]{2,1,0:T(1,128)S(1)} %broadcast_in_dim.7), channel_id=1, replica_groups=mesh['yh'=2,'x'=4,'z'=8,'yl'=4,'c'=2] {'yl','c'}, dimensions={0} | all-to-all | bytes 73728 | tf_op jit(solution)/shard_map/all_to_all | solution.py:237
  72.3 0.1 broadcast_in_dim.16
  72.4 14.3 %all_to_all.23.small_ref = f32[32,1,1152]{2,1,0:T(1,128)S(1)} all-to-all(f32[32,1,1152]{2,1,0:T(1,128)S(1)} %broadcast_in_dim.16), channel_id=1, replica_groups=mesh['yh'=2,'x'=4,'z'=8,'yl'=4,'c'=2] {'x','z'}, dimensions={0} | all-to-all | bytes 294912 | tf_op jit(solution)/shard_map/all_to_all | solution.py:237
  86.7 0.0 copy-done.1
  86.7 0.8 shard_map.79
  (4 shorter events, 0.1 us)
Async XLA Ops:
  31.3 14.4 %copy-start = (f32[16,512]{1,0:T(8,128)S(1)}, f32[16,512]{1,0:T(8,128)}, u32[]{:S(2)}) copy-start(f32[16,512]{1,0:T(8,128)} %weight_ref.3) | copy-start | bytes 98308
  31.3 14.4 %copy-start.2 = (f32[16]{0:T(128)S(1)}, f32[16]{0:T(128)}, u32[]{:S(2)}) copy-start(f32[16]{0:T(128)} %param.8) | copy-start | bytes 196
  31.3 55.4 %copy-start.1 = (f32[512]{0:T(512)S(1)}, f32[512]{0:T(512)}, u32[]{:S(2)}) copy-start(f32[512]{0:T(512)} %param.9) | copy-start | bytes 6148
  45.8 9.3 %collective-permute-start = (f32[40,512]{1,0:T(8,128)S(1)}, f32[40,512]{1,0:T(8,128)S(1)}, u32[]{:S(2)}, u32[]{:S(2)}) collective-permute-start(f32[40,512]{1,0:T(8,128)S(1)} %shard_map.77.mine_ref), channel_id=1, source_target_pairs={{0,256},{256,0},{1,257},{257,1},{2,258},{258,2},{3,259},{259,3},{4... | collective-permute-start | bytes 245768 | tf_op jit(solution)/shard_map/ppermute | solution.py:246

commit v2 on v1

--- a/solution.py
+++ b/solution.py
@@ -245,8 +245,8 @@
     mine = pack(parts, weight, row_moment.reshape(1, ROWS))
     other = lax.ppermute(mine, "yh", [(0, 1), (1, 0)])
     grad, row_values, small = statistics(mine, other)
-    small = jnp.sum(copies_of(small, ("yl", "c"), 8), axis=0)
-    small = copies_of(small, ("x", "z"), 32)
+    small = jnp.sum(copies_of(small, ("c", "z"), 16), axis=0)
+    small = copies_of(small, ("x", "yl"), 16)
     new_weight, new_rows, new_cols = apply_update(small, grad, row_values, weight, col_moment.reshape(1, WIDTH))
     return (new_weight, new_rows.reshape(ROWS), new_cols.reshape(WIDTH))
 

time: 87.8 us -> 87.6 us (level)
  no operation moved by 1% of the time
where the time goes in v2:
time: 87.6 us; the launch traced here: 87.3 us
  blocking collectives  72.2 us (82%)
  starting transfers between devices  7.41 us (8%)
  Pallas kernels  4.73 us (5%)
  waiting for transfers between devices  1.9 us (2%)
    all_to_all x2, blocking collectives, copies_of(): lax.all_to_all(jnp.broadcast_to(value[None], (count,) + value.shape), axe...  31 us
    all_to_all x1, blocking collectives, body(): lax.all_to_all(parts, AXES, 0, 0, tiled=True, axis_index_groups=near_grou...  26.9 us
    all_to_all x1, blocking collectives, body(): lax.all_to_all(parts, AXES, 0, 0, tiled=True, axis_index_groups=far_group...  14.2 us
    ppermute x1, starting transfers between devices, body(): other = lax.ppermute(mine, 'yh', [(0, 1), (1, 0)])  7.41 us
    pallas_call x1, Pallas kernels, token_product(): pl.pallas_call(product_kernel, in_specs=[pl.BlockSpec(memory_space=pl.ANY...  3.71 us
    ppermute x1, waiting for transfers between devices, body(): other = lax.ppermute(mine, 'yh', [(0, 1), (1, 0)])  1.9 us
  transfers between devices with their start and end apart: 1, of which 1 were waited for; matrix products, arithmetic and copies ran while one was open for 0% of the time, Pallas kernels for 0%

profile of v2, /device:TPU:1, one launch (start us, length us, event | category | flops | bytes accessed | tf_op | source)
XLA Modules:
  0.0 87.3 jit_solution(8919028858708234296)
XLA Ops:
  0.6 3.7 %shard_map.76 = f32[4,16,16,512]{3,2,1,0:T(8,128)S(1)} custom-call(bf16[1664,1024]{1,0:T(8,128)(2,1)} %inputs_ref.1, bf16[1664,512]{1,0:T(8,128)(2,1)} %columns_ref.1), custom_call_target="tpu_custom_call" | custom-call | tf_op jit(solution)/shard_map/pallas_call | solution.py:121
  4.3 26.9 %all_to_all.20 = f32[4,16,16,512]{3,2,1,0:T(8,128)S(1)} all-to-all(f32[4,16,16,512]{3,2,1,0:T(8,128)S(1)} %shard_map.76), channel_id=1, replica_groups={{72,64,8,0},{145,137,81,73},{74,66,10,2},{147,139,83,75},{76,68,12,4},{..., dimensions={0} | all-to-all | bytes 4194304 | tf_op jit(solution)/shard_map/all_to_all | solution.py:242
  31.3 0.0 copy-start
  31.3 0.0 copy-start.2
  31.3 0.0 copy-start.1
  31.3 0.3 reduce_sum.18
  31.5 14.2 %all_to_all.21.parts_ref = f32[8,2,16,512]{3,2,1,0:T(8,128)S(1)} all-to-all(f32[8,2,16,512]{3,2,1,0:T(8,128)S(1)} %bitcast.7), channel_id=1, replica_groups={{72,88,96,112,136,152,160,176},{145,161,169,185,209,225,233,249},{74,90..., dimensions={0} | all-to-all | bytes 1048576 | tf_op jit(solution)/shard_map/all_to_all | solution.py:244
  45.7 0.0 copy-done
  45.7 0.0 copy-done.2
  45.8 7.4 %collective-permute-start = (f32[40,512]{1,0:T(8,128)S(1)}, f32[40,512]{1,0:T(8,128)S(1)}, u32[]{:S(2)}, u32[]{:S(2)}) collective-permute-start(f32[40,512]{1,0:T(8,128)S(1)} %shard_map.77.mine_ref), channel_id=1, source_target_pairs={{0,256},{256,0},{1,257},{257,1},{2,258},{258,2},{3,259},{259,3},{4... | collective-permute-start | bytes 245768 | tf_op jit(solution)/shard_map/ppermute | solution.py:246
  53.2 1.9 %collective-permute-done.other_ref = f32[40,512]{1,0:T(8,128)S(1)} collective-permute-done((f32[40,512]{1,0:T(8,128)S(1)}, f32[40,512]{1,0:T(8,128)S(1)}, u32[]{:S(2)}, u32[]{:S(2)}) %collective-permute-start) | collective-permute-done | bytes 81952 | tf_op jit(solution)/shard_map/ppermute | solution.py:246
  55.1 0.2 shard_map.78
  55.3 19.6 %all_to_all.22 = f32[16,1,1152]{2,1,0:T(1,128)S(1)} all-to-all(f32[16,1,1152]{2,1,0:T(1,128)S(1)} %broadcast_in_dim.7), channel_id=1, replica_groups=mesh['yh'=2,'x'=4,'z'=8,'yl'=4,'c'=2] {'c','z'}, dimensions={0} | all-to-all | bytes 147456 | tf_op jit(solution)/shard_map/all_to_all | solution.py:237
  75.0 0.1 reduce_sum.19
  75.1 11.4 %all_to_all.23.small_ref = f32[16,1,1152]{2,1,0:T(1,128)S(1)} all-to-all(f32[16,1,1152]{2,1,0:T(1,128)S(1)} %broadcast_in_dim.16), channel_id=1, replica_groups=mesh['yh'=2,'x'=4,'z'=8,'yl'=4,'c'=2] {'x','yl'}, dimensions={0} | all-to-all | bytes 147456 | tf_op jit(solution)/shard_map/all_to_all | solution.py:237
  86.5 0.0 copy-done.1
  86.5 0.8 shard_map.79
  (4 shorter events, 0.1 us)
Async XLA Ops:
  31.3 14.4 %copy-start = (f32[16,512]{1,0:T(8,128)S(1)}, f32[16,512]{1,0:T(8,128)}, u32[]{:S(2)}) copy-start(f32[16,512]{1,0:T(8,128)} %weight_ref.3) | copy-start | bytes 98308
  31.3 14.4 %copy-start.2 = (f32[16]{0:T(128)S(1)}, f32[16]{0:T(128)}, u32[]{:S(2)}) copy-start(f32[16]{0:T(128)} %param.8) | copy-start | bytes 196
  31.3 55.2 %copy-start.1 = (f32[512]{0:T(512)S(1)}, f32[512]{0:T(512)}, u32[]{:S(2)}) copy-start(f32[512]{0:T(512)} %param.9) | copy-start | bytes 6148
  45.8 9.3 %collective-permute-start = (f32[40,512]{1,0:T(8,128)S(1)}, f32[40,512]{1,0:T(8,128)S(1)}, u32[]{:S(2)}, u32[]{:S(2)}) collective-permute-start(f32[40,512]{1,0:T(8,128)S(1)} %shard_map.77.mine_ref), channel_id=1, source_target_pairs={{0,256},{256,0},{1,257},{257,1},{2,258},{258,2},{3,259},{259,3},{4... | collective-permute-start | bytes 245768 | tf_op jit(solution)/shard_map/ppermute | solution.py:246
